TPU v7x, 256 devices: a whole 4x4x8 slice. The times are simulated.
256 devices in a mesh: prow: 16 (over z, core), pcol: 16 (over x, y).
Axes of the slice: x: 4, y: 4, z: 8, core: 2. Of those that a mesh axis runs over, the one named last changes fastest.
Arguments:
- leaf_source: bfloat16 [16, 16, 8, 256, 128], P('prow', 'pcol'), may hold values from -6 to 6
- band_source: bfloat16 [16, 256, 128], P('prow'), may hold values from -6 to 6
- strip_source: bfloat16 [16, 256, 128], P('pcol'), may hold values from -6 to 6
- summit_source: bfloat16 [256, 128], replicated, may hold values from -6 to 6
- leaf_inverse: bfloat16 [16, 16, 8, 256, 256], P('prow', 'pcol'), may hold values from -1 to 2
- band_inverse: bfloat16 [16, 256, 256], P('prow'), may hold values from -1 to 2
- strip_inverse: bfloat16 [16, 256, 256], P('pcol'), may hold values from -1 to 2
- summit_inverse: bfloat16 [256, 256], replicated, may hold values from -1 to 2
- leaf_blocks: bfloat16 [16, 16, 28, 256, 256], P('prow', 'pcol'), may hold values from -0.09375 to 0.09375
- band_blocks: bfloat16 [16, 16, 8, 256, 256], P('prow', 'pcol'), may hold values from -0.0234375 to 0.0234375
- strip_blocks: bfloat16 [16, 16, 8, 256, 256], P('prow', 'pcol'), may hold values from -0.0234375 to 0.0234375
- summit_blocks: bfloat16 [16, 16, 8, 256, 256], P('prow', 'pcol'), may hold values from -0.015625 to 0.015625
- coupling: bfloat16 [16, 16, 256, 256], P('prow', 'pcol'), may hold values from -0.0625 to 0.0625
- summit_band: bfloat16 [16, 256, 256], P('prow', 'pcol'), may hold values from -0.046875 to 0.046875
- summit_strip: bfloat16 [16, 256, 256], P('pcol'), may hold values from -0.046875 to 0.046875
- parents: int32 [16, 16, 8], P('prow', 'pcol'), may hold values from 1 to 8, as said below
- widths: int32 [16, 16, 8], P('prow', 'pcol'), may hold values from 64 to 256
Outputs:
- leaf_answer: bfloat16 [16, 16, 8, 256, 128], P('prow', 'pcol')
- band_answer: bfloat16 [16, 256, 128], P('prow')
- strip_answer: bfloat16 [16, 256, 128], P('pcol')
- summit_answer: bfloat16 [256, 128], replicated
Inputs may be any that keep to these rules, and one draw needn't show every extreme that they name: parents[r, c, a] is a later leaf of the same subtree, or 8 where leaf a links only to the separators.
All inputs are finite; a program needn't handle non-finite values.
Results may differ from a plain program's by a relative error of at most 0.015.
Values sent between devices are 32-bit elements; how exact they have to be, the bound alone decides.
A program may use at most 64 MiB of HBM per device.

v0:
```python
import jax
import jax.numpy as jnp
from jax import lax
from jax.sharding import PartitionSpec as P

PASSES = 2


def ancestors(parent_list, leaf_count):
    node_ids = jnp.arange(leaf_count + 1, dtype=jnp.int32)
    current = parent_list
    extended = jnp.concatenate([current, jnp.full((1,), leaf_count, jnp.int32)])
    reached = jnp.zeros((leaf_count + 1, leaf_count), jnp.float32)
    for repeat in range(leaf_count):
        matches = current[None, :] == node_ids[:, None]
        reached = jnp.maximum(reached, matches.astype(jnp.float32))
        current = jnp.sum(jnp.where(matches, extended[:, None], 0), axis=0)
    return reached[:leaf_count]


def multiply(left, right, form):
    return jnp.einsum(form, left, right, preferred_element_type=jnp.float32)


def forward_block(inverse, source, partial_value):
    residual = (source.astype(jnp.float32) - partial_value).astype(jnp.bfloat16)
    return multiply(inverse, residual, "ij,jr->ir").astype(jnp.bfloat16)


def backward_block(inverse, source, partial_value):
    residual = (source.astype(jnp.float32) - partial_value).astype(jnp.bfloat16)
    return multiply(inverse, residual, "ji,jr->ir").astype(jnp.bfloat16)


def leaf_forward(pair_blocks, inverses, sources, reached, row_mask):
    leaf_count = sources.shape[0]
    solved = []
    for position in range(leaf_count):
        residual = sources[position].astype(jnp.float32)
        if position > 0:
            first_pair = position * (position - 1) // 2
            weights = reached[position, :position].astype(jnp.bfloat16)
            stacked = jnp.stack(solved) * weights[:, None, None]
            residual = residual - multiply(
                pair_blocks[first_pair : first_pair + position], stacked, "bij,bjr->ir"
            )
        residual = (row_mask[position] * residual).astype(jnp.bfloat16)
        solved.append(
            (row_mask[position] * multiply(inverses[position], residual, "ij,jr->ir")).astype(
                jnp.bfloat16
            )
        )
    return jnp.stack(solved)


def leaf_backward(pair_blocks, inverses, solved, outer, reached, row_mask):
    leaf_count = solved.shape[0]
    pending = outer
    answers = [None] * leaf_count
    for position in reversed(range(leaf_count)):
        residual = (
            row_mask[position] * (solved[position].astype(jnp.float32) - pending[position])
        ).astype(jnp.bfloat16)
        update = (row_mask[position] * multiply(inverses[position], residual, "ji,jr->ir")).astype(
            jnp.bfloat16
        )
        answers[position] = update
        if position > 0:
            first_pair = position * (position - 1) // 2
            pushed = multiply(
                pair_blocks[first_pair : first_pair + position], update, "bji,jr->bir"
            )
            pending = pending.at[:position].add(
                reached[position, :position][:, None, None] * pushed
            )
    return jnp.stack(answers)


def per_device(
    leaf_source,
    band_source,
    strip_source,
    summit_source,
    leaf_inverse,
    band_inverse,
    strip_inverse,
    summit_inverse,
    leaf_blocks,
    band_blocks,
    strip_blocks,
    summit_blocks,
    coupling,
    summit_band,
    summit_strip,
    parents,
    widths,
):
    leaf_count = leaf_source.shape[2]
    block_width = leaf_source.shape[3]
    reached = ancestors(parents[0, 0], leaf_count)
    column_ids = jnp.arange(block_width, dtype=jnp.int32)
    row_mask = (column_ids[None, :] < widths[0, 0][:, None]).astype(jnp.float32)[:, :, None]
    band_slab = summit_band.shape[1]
    strip_slab = block_width // lax.axis_size("prow")
    column_place = lax.axis_index("pcol") * band_slab
    row_place = lax.axis_index("prow") * strip_slab
    inverses = leaf_inverse[0, 0]
    pair_blocks = leaf_blocks[0, 0]
    to_band = band_blocks[0, 0]
    to_strip = strip_blocks[0, 0]
    to_summit = summit_blocks[0, 0]
    link_block = coupling[0, 0]
    lift_band = summit_band[0]
    lift_strip = summit_strip[0]
    current = (leaf_source[0, 0], band_source[0], strip_source[0], summit_source)
    for iteration in range(PASSES):
        leaf_now, band_now, strip_now, summit_now = current
        solved = leaf_forward(pair_blocks, inverses, leaf_now, reached, row_mask)
        band_term = multiply(to_band, solved, "aij,ajr->ir")
        strip_term = multiply(to_strip, solved, "aij,ajr->ir")
        summit_term = multiply(to_summit, solved, "aij,ajr->ir")
        band_partial = lax.psum(band_term, "pcol")
        band_solved = forward_block(band_inverse[0], band_now, band_partial)
        own_band = lax.dynamic_slice_in_dim(band_solved, column_place, band_slab, 0)
        summit_term = summit_term + multiply(lift_band, own_band, "ki,kn->in")
        strip_term = strip_term + multiply(link_block, band_solved, "ij,jn->in")
        strip_partial = lax.psum(strip_term, "prow")
        strip_solved = forward_block(strip_inverse[0], strip_now, strip_partial)
        own_lift = lax.dynamic_slice_in_dim(lift_strip, row_place, strip_slab, 0)
        own_strip = lax.dynamic_slice_in_dim(strip_solved, row_place, strip_slab, 0)
        summit_partial = lax.psum(
            summit_term + multiply(own_lift, own_strip, "ki,kn->in"), ("prow", "pcol")
        )
        summit_solved = forward_block(summit_inverse, summit_now, summit_partial)
        summit_answer = backward_block(
            summit_inverse, summit_solved, jnp.zeros(summit_solved.shape, jnp.float32)
        )
        strip_answer = backward_block(
            strip_inverse[0], strip_solved, multiply(lift_strip, summit_answer, "ki,in->kn")
        )
        downward = multiply(link_block, strip_answer, "ji,jn->in")
        band_piece = multiply(lift_band, summit_answer, "ki,in->kn")
        band_back = lax.psum(downward, "pcol") + lax.all_gather(
            band_piece, "pcol", axis=0, tiled=True
        )
        band_answer = backward_block(band_inverse[0], band_solved, band_back)
        outer = (
            multiply(to_band, band_answer, "aij,ir->ajr")
            + multiply(to_strip, strip_answer, "aij,ir->ajr")
            + multiply(to_summit, summit_answer, "aij,ir->ajr")
        )
        leaf_answer = leaf_backward(pair_blocks, inverses, solved, outer, reached, row_mask)
        current = (leaf_answer, band_answer, strip_answer, summit_answer)
    return (current[0][None, None], current[1][None], current[2][None], current[3])


def solution(mesh):
    placed = (
        P("prow", "pcol", None, None, None),
        P("prow", None, None),
        P("pcol", None, None),
        P(),
        P("prow", "pcol", None, None, None),
        P("prow", None, None),
        P("pcol", None, None),
        P(),
        P("prow", "pcol", None, None, None),
        P("prow", "pcol", None, None, None),
        P("prow", "pcol", None, None, None),
        P("prow", "pcol", None, None, None),
        P("prow", "pcol", None, None),
        P("prow", "pcol", None),
        P("pcol", None, None),
        P("prow", "pcol", None),
        P("prow", "pcol", None),
    )
    return jax.shard_map(
        per_device,
        mesh=mesh,
        in_specs=placed,
        out_specs=(
            P("prow", "pcol", None, None, None),
            P("prow", None, None),
            P("pcol", None, None),
            P(),
        ),
        check_vma=False,
    )
```

profile of v0, /device:TPU:2, one launch (start us, length us, event | category | flops | bytes accessed | tf_op | source)
XLA Modules:
  0.0 1181.8 jit_solution(3843605746356094015)
XLA Ops:
  14.1 1.9 constant_dynamic-update-slice_fusion.17
  15.9 2.0 constant_dynamic-update-slice_fusion.16
  17.9 2.1 constant_dynamic-update-slice_fusion.15
  20.0 2.1 constant_dynamic-update-slice_fusion.14
  22.1 2.2 constant_dynamic-update-slice_fusion.13
  25.3 2.5 constant_dynamic-update-slice_fusion.12
  28.6 2.6 constant_dynamic-update-slice_fusion.11
  31.2 2.6 constant_dynamic-update-slice_fusion.18
  33.8 2.2 convolution_bitcast_fusion.19
  42.3 2.1 convolution_bitcast_fusion.17
  44.4 2.1 convolution_bitcast_fusion.18
  46.5 84.6 %all-reduce.9.cloned.1.call-done = f32[256,128]{1,0:T(8,128)} async-done(((f32[256,128]{1,0:T(8,128)}), f32[256,128]{1,0:T(8,128)}) %all-reduce.9.cloned.1.call-update) | async-done | bytes 131088 | tf_op jit(solution)/shard_map/psum | solution.py:122
  133.0 1.7 fusion.29
  134.8 1.8 fusion.34
  136.7 105.3 %all-reduce.11.cloned.1.call-done = f32[256,128]{1,0:T(8,128)} async-done(((f32[256,128]{1,0:T(8,128)}), f32[256,128]{1,0:T(8,128)}) %all-reduce.11.cloned.1.call-update) | async-done | bytes 131088 | tf_op jit(solution)/shard_map/psum | solution.py:127
  243.8 1.8 convolution_add_fusion.8
  246.8 243.6 %all-reduce.13.cloned.1.call-done = f32[256,128]{1,0:T(8,128)} async-done(((f32[256,128]{1,0:T(8,128)}), f32[256,128]{1,0:T(8,128)}) %all-reduce.13.cloned.1.call-update) | async-done | bytes 131088 | tf_op jit(solution)/shard_map/psum | solution.py:131
  490.5 1.9 convolution_convert_fusion.8
  492.3 1.9 convolution_convert_fusion.7
  494.2 1.7 convolution_bitcast_fusion.10
  496.9 23.8 %all_gather.6 = f32[256,128]{1,0:T(8,128)} all-gather(f32[16,128]{1,0:T(8,128)S(1)} %convolution_bitcast_fusion.22), channel_id=1, replica_groups=mesh['prow'=16,'pcol'=16] {'pcol'}, dimensions={0}, use_global_device_ids=true | all-gather | bytes 139264 | tf_op jit(solution)/shard_map/all_gather | solution.py:143
  520.7 1.6 copy.39
  522.3 62.3 %all-reduce.15.cloned.1.call-done = f32[256,128]{0,1:T(8,128)} async-done(((f32[256,128]{0,1:T(8,128)}), f32[256,128]{0,1:T(8,128)}) %all-reduce.15.cloned.1.call-update) | async-done | bytes 131088 | tf_op jit(solution)/shard_map/psum | solution.py:143
  593.4 1.5 fusion.77
  594.9 2.0 constant_dynamic-update-slice_fusion.43
  596.9 2.1 constant_dynamic-update-slice_fusion.42
  599.0 2.2 constant_dynamic-update-slice_fusion.41
  601.2 2.4 constant_dynamic-update-slice_fusion.40
  603.6 2.4 constant_dynamic-update-slice_fusion.39
  606.0 2.5 constant_dynamic-update-slice_fusion.38
  608.5 2.6 constant_dynamic-update-slice_fusion.37
  611.1 2.7 constant_dynamic-update-slice_fusion.44
  613.8 2.2 convolution_bitcast_fusion.13
  616.0 2.2 convolution_bitcast_fusion.15
  618.2 2.2 convolution_bitcast_fusion.14
  620.4 89.7 %all-reduce.17.cloned.1.call-done = f32[256,128]{0,1:T(8,128)} async-done(((f32[256,128]{0,1:T(8,128)}), f32[256,128]{0,1:T(8,128)}) %all-reduce.17.cloned.1.call-update) | async-done | bytes 131088 | tf_op jit(solution)/shard_map/psum | solution.py:122
  712.0 1.8 fusion.27
  713.8 1.8 fusion.33
  715.6 105.4 %all-reduce.19.cloned.1.call-done = f32[256,128]{0,1:T(8,128)} async-done(((f32[256,128]{0,1:T(8,128)}), f32[256,128]{0,1:T(8,128)}) %all-reduce.19.cloned.1.call-update) | async-done | bytes 131088 | tf_op jit(solution)/shard_map/psum | solution.py:127
  822.8 1.8 convolution_add_fusion.6
  824.6 245.8 %all-reduce.21.cloned.1.call-done = f32[256,128]{0,1:T(8,128)} async-done(((f32[256,128]{0,1:T(8,128)}), f32[256,128]{0,1:T(8,128)}) %all-reduce.21.cloned.1.call-update) | async-done | bytes 131088 | tf_op jit(solution)/shard_map/psum | solution.py:131
  1070.4 1.9 convolution_convert_fusion.2
  1075.4 1.6 copy.44
  1077.7 22.2 %all_gather.7 = f32[256,128]{1,0:T(8,128)S(1)} all-gather(f32[16,128]{1,0:T(8,128)S(1)} %convolution_bitcast_fusion.21), channel_id=1, replica_groups=mesh['prow'=16,'pcol'=16] {'pcol'}, dimensions={0}, use_global_device_ids=true | all-gather | bytes 139264 | tf_op jit(solution)/shard_map/all_gather | solution.py:143
  1100.7 62.5 %all-reduce.23.cloned.1.call-done = f32[256,128]{0,1:T(8,128)} async-done(((f32[256,128]{0,1:T(8,128)}), f32[256,128]{0,1:T(8,128)}) %all-reduce.23.cloned.1.call-update) | async-done | bytes 131088 | tf_op jit(solution)/shard_map/psum | solution.py:143
  1164.4 1.3 fusion.130
  1166.4 1.7 convolution_add_fusion.1
  1171.9 2.0 fusion.121
  (269 shorter events, 42.9 us)
Async XLA Ops:
  7.2 26.6 %copy-start = (bf16[1,1,8,256,256]{4,3,2,1,0:T(8,128)(2,1)S(1)}, bf16[1,1,8,256,256]{4,3,2,1,0:T(8,128)(2,1)}, u32[]{:S(2)}) copy-start(bf16[1,1,8,256,256]{4,3,2,1,0:T(8,128)(2,1)} %param.54) | copy-start | bytes 3145732
  7.2 124.0 %all-reduce.9.cloned.1.call-start = ((), (), s32[]{:S(2)}) async-start(), calls=%async_computation | async-start | bytes 262144 | tf_op jit(solution)/shard_map/psum | solution.py:122
  10.6 20.6 %copy-start.79 = (bf16[7]{0:T(256)(128)(2,1)}, bf16[7]{0:T(256)(128)(2,1)S(1)}, u32[]{:S(2)}) copy-start(bf16[7]{0:T(256)(128)(2,1)S(1)} %fusion.590) | copy-start | bytes 46
  10.6 18.0 %copy-start.80 = (bf16[6]{0:T(256)(128)(2,1)}, bf16[6]{0:T(256)(128)(2,1)S(1)}, u32[]{:S(2)}) copy-start(bf16[6]{0:T(256)(128)(2,1)S(1)} %fusion.589) | copy-start | bytes 40
  10.6 14.7 %copy-start.81 = (bf16[5]{0:T(256)(128)(2,1)}, bf16[5]{0:T(256)(128)(2,1)S(1)}, u32[]{:S(2)}) copy-start(bf16[5]{0:T(256)(128)(2,1)S(1)} %fusion.588) | copy-start | bytes 34
  10.7 13.6 %copy-start.82 = (bf16[4]{0:T(256)(128)(2,1)}, bf16[4]{0:T(256)(128)(2,1)S(1)}, u32[]{:S(2)}) copy-start(bf16[4]{0:T(256)(128)(2,1)S(1)} %fusion.587) | copy-start | bytes 28
  10.7 13.6 %copy-start.83 = (bf16[3]{0:T(256)(128)(2,1)}, bf16[3]{0:T(256)(128)(2,1)S(1)}, u32[]{:S(2)}) copy-start(bf16[3]{0:T(256)(128)(2,1)S(1)} %fusion.586) | copy-start | bytes 22
  10.7 13.6 %copy-start.84 = (bf16[2]{0:T(256)(128)(2,1)}, bf16[2]{0:T(256)(128)(2,1)S(1)}, u32[]{:S(2)}) copy-start(bf16[2]{0:T(256)(128)(2,1)S(1)} %fusion.585) | copy-start | bytes 16
  12.1 12.2 %copy-start.45 = (f32[1,256]{1,0:T(1,128)}, f32[1,256]{1,0:T(1,128)S(1)}, u32[]{:S(2)}) copy-start(f32[1,256]{1,0:T(1,128)S(1)} %get-tuple-element.241) | copy-start | bytes 3076
  12.2 12.2 %copy-start.48 = (f32[1,256]{1,0:T(1,128)}, f32[1,256]{1,0:T(1,128)S(1)}, u32[]{:S(2)}) copy-start(f32[1,256]{1,0:T(1,128)S(1)} %get-tuple-element.240) | copy-start | bytes 3076
  12.2 12.2 %copy-start.61 = (f32[1,256]{1,0:T(1,128)}, f32[1,256]{1,0:T(1,128)S(1)}, u32[]{:S(2)}) copy-start(f32[1,256]{1,0:T(1,128)S(1)} %get-tuple-element.244) | copy-start | bytes 3076
  12.2 13.1 %copy-start.51 = (f32[1,256]{1,0:T(1,128)}, f32[1,256]{1,0:T(1,128)S(1)}, u32[]{:S(2)}) copy-start(f32[1,256]{1,0:T(1,128)S(1)} %get-tuple-element.239) | copy-start | bytes 3076
  12.2 16.4 %copy-start.54 = (f32[1,256]{1,0:T(1,128)}, f32[1,256]{1,0:T(1,128)S(1)}, u32[]{:S(2)}) copy-start(f32[1,256]{1,0:T(1,128)S(1)} %get-tuple-element.238) | copy-start | bytes 3076
  12.2 19.0 %copy-start.57 = (f32[1,256]{1,0:T(1,128)}, f32[1,256]{1,0:T(1,128)S(1)}, u32[]{:S(2)}) copy-start(f32[1,256]{1,0:T(1,128)S(1)} %get-tuple-element.237) | copy-start | bytes 3076
  15.9 11.8 %copy-start.26 = (bf16[128,256]{1,0:T(8,128)(2,1)}, bf16[128,256]{1,0:T(8,128)(2,1)S(1)}, u32[]{:S(2)}) copy-start(bf16[128,256]{1,0:T(8,128)(2,1)S(1)} %get-tuple-element.245) | copy-start | bytes 196612
  17.9 9.9 copy-start.28
  20.0 7.8 copy-start.31
  22.1 5.7 copy-start.34
  25.3 17.0 %copy-start.2 = (bf16[1,1,8,256,256]{4,3,2,1,0:T(8,128)(2,1)S(1)}, bf16[1,1,8,256,256]{4,3,2,1,0:T(8,128)(2,1)}, u32[]{:S(2)}) copy-start(bf16[1,1,8,256,256]{4,3,2,1,0:T(8,128)(2,1)} %param.56) | copy-start | bytes 3145732
  28.6 15.8 %copy-start.1 = (bf16[1,1,8,256,256]{4,3,2,1,0:T(8,128)(2,1)S(1)}, bf16[1,1,8,256,256]{4,3,2,1,0:T(8,128)(2,1)}, u32[]{:S(2)}) copy-start(bf16[1,1,8,256,256]{4,3,2,1,0:T(8,128)(2,1)} %param.55) | copy-start | bytes 3145732
  31.2 101.8 %copy-start.9 = (bf16[1,1,256,256]{3,2,1,0:T(8,128)(2,1)S(1)}, bf16[1,1,256,256]{3,2,1,0:T(8,128)(2,1)}, u32[]{:S(2)}) copy-start(bf16[1,1,256,256]{3,2,1,0:T(8,128)(2,1)} %param.57) | copy-start | bytes 393220
  33.8 101.0 %copy-start.25 = (bf16[1,16,256]{2,1,0:T(8,128)(2,1)S(1)}, bf16[1,16,256]{2,1,0:T(8,128)(2,1)}, u32[]{:S(2)}) copy-start(bf16[1,16,256]{2,1,0:T(8,128)(2,1)} %param.58) | copy-start | bytes 24580
  33.8 208.2 %copy-start.8 = (bf16[1,256,256]{2,1,0:T(8,128)(2,1)S(1)}, bf16[1,256,256]{2,1,0:T(8,128)(2,1)}, u32[]{:S(2)}) copy-start(bf16[1,256,256]{2,1,0:T(8,128)(2,1)} %param.51) | copy-start | bytes 393220
  33.8 456.7 %copy-start.10 = (bf16[256,256]{1,0:T(8,128)(2,1)S(1)}, bf16[256,256]{1,0:T(8,128)(2,1)}, u32[]{:S(2)}) copy-start(bf16[256,256]{1,0:T(8,128)(2,1)} %param.52) | copy-start | bytes 393220
  36.0 206.0 %all-reduce.11.cloned.1.call-start = ((), (), s32[]{:S(2)}) async-start(), calls=%async_computation.1 | async-start | bytes 262144 | tf_op jit(solution)/shard_map/psum | solution.py:127
  134.8 355.7 %all-reduce.13.cloned.1.call-start = ((), (), s32[]{:S(2)}) async-start(), calls=%async_computation.2 | async-start | bytes 262144 | tf_op jit(solution)/shard_map/psum | solution.py:131
  245.6 339.0 %all-reduce.15.cloned.1.call-start = ((), (), s32[]{:S(2)}) async-start(), calls=%async_computation.3 | async-start | bytes 262144 | tf_op jit(solution)/shard_map/psum | solution.py:143
  495.9 214.2 %all-reduce.17.cloned.1.call-start = ((), (), s32[]{:S(2)}) async-start(), calls=%async_computation.4 | async-start | bytes 262144 | tf_op jit(solution)/shard_map/psum | solution.py:122
  584.6 3.6 copy-start.12
  586.8 2.4 copy-start.3
  586.9 2.4 copy-start.70
  588.5 1.9 copy-start.38
  588.6 2.0 copy-start.68
  589.8 2.4 copy-start.32
  590.4 1.9 copy-start.72
  590.4 2.2 copy-start.29
  590.6 2.2 copy-start.19
  590.6 2.8 copy-start.27
  590.6 2.8 copy-start.62
  618.2 202.9 %all-reduce.19.cloned.1.call-start = ((), (), s32[]{:S(2)}) async-start(), calls=%async_computation.5 | async-start | bytes 262144 | tf_op jit(solution)/shard_map/psum | solution.py:127
  713.8 356.7 %all-reduce.21.cloned.1.call-start = ((), (), s32[]{:S(2)}) async-start(), calls=%async_computation.6 | async-start | bytes 262144 | tf_op jit(solution)/shard_map/psum | solution.py:131
  824.6 338.6 %all-reduce.23.cloned.1.call-start = ((), (), s32[]{:S(2)}) async-start(), calls=%async_computation.7 | async-start | bytes 262144 | tf_op jit(solution)/shard_map/psum | solution.py:143
  1073.5 94.6 %copy-start.11 = (bf16[128,256]{1,0:T(8,128)(2,1)S(1)}, bf16[128,256]{1,0:T(8,128)(2,1)}, u32[]{:S(2)}) copy-start(bf16[128,256]{1,0:T(8,128)(2,1)} %convolution_convert_fusion.2) | copy-start | bytes 196612
  1165.7 2.8 copy-start.44
  1165.7 2.8 copy-start.59
  1165.7 3.0 copy-start.71
  1166.4 2.1 copy-start.7
  1166.4 2.7 copy-start.4
  (45 other events, 60.7 us)
Sparse Core Ops, SparseCore 0:
  36.1 94.9 all-reduce.8
  134.9 107.0 all-reduce.10
  248.1 242.3 all-reduce.12
  496.0 88.5 all-reduce.14
  618.3 91.8 all-reduce.16
  713.9 107.1 all-reduce.18
  828.0 242.3 all-reduce.20
  1074.5 88.5 all-reduce.22
where the time goes:
time: 1180 us
  waiting for transfers between devices  999 us (85%)
  matrix products  92.7 us (8%)
  blocking collectives  46 us (4%)
  local copies, waits for them, and re-layouts  23.6 us (2%)
  between operations  16.2 us (1%)
    psum x2, waiting for transfers between devices, per_device(): lax.psum(summit_term + multiply(own_lift, own_strip, 'ki,kn->in'), ('prow...  489 us
    psum x2, waiting for transfers between devices, per_device(): strip_partial = lax.psum(strip_term, 'prow')  211 us
    psum x2, waiting for transfers between devices, per_device(): band_partial = lax.psum(band_term, 'pcol')  174 us
    psum x2, waiting for transfers between devices, per_device(): lax.psum(downward, 'pcol')  125 us
    dot_general x76, matrix products, multiply(): return jnp.einsum(form, left, right, preferred_element_type=jnp.float32)  92.7 us
    all_gather x2, blocking collectives, per_device(): lax.all_gather(band_piece, 'pcol', axis=0, tiled=True)  46 us
  transfers between devices with their start and end apart: 8, of which 8 were waited for; matrix products, arithmetic and copies ran while one was open for 2% of the time, Pallas kernels for 0%

commit v1 on v0

--- a/solution.py
+++ b/solution.py
@@ -4,6 +4,24 @@
 from jax.sharding import PartitionSpec as P
 
 PASSES = 2
+
+
+def collect(shard, axis, dim):
+    ways, here, step = (lax.axis_size(axis), lax.axis_index(axis), shard.shape[dim])
+    dims = [n * ways if d == dim else n for d, n in enumerate(shard.shape)]
+    full = lax.dynamic_update_slice_in_dim(
+        jnp.zeros(dims, shard.dtype), shard, here * step, axis=dim
+    )
+    going_up = going_down = shard
+    for far in range(1, ways // 2 + 1):
+        going_up = lax.ppermute(going_up, axis, [(d, (d + 1) % ways) for d in range(ways)])
+        full = lax.dynamic_update_slice_in_dim(full, going_up, (here - far) % ways * step, axis=dim)
+        if 2 * far < ways:
+            going_down = lax.ppermute(going_down, axis, [(d, (d - 1) % ways) for d in range(ways)])
+            full = lax.dynamic_update_slice_in_dim(
+                full, going_down, (here + far) % ways * step, axis=dim
+            )
+    return full
 
 
 def ancestors(parent_list, leaf_count):
@@ -140,9 +158,7 @@
         )
         downward = multiply(link_block, strip_answer, "ji,jn->in")
         band_piece = multiply(lift_band, summit_answer, "ki,in->kn")
-        band_back = lax.psum(downward, "pcol") + lax.all_gather(
-            band_piece, "pcol", axis=0, tiled=True
-        )
+        band_back = lax.psum(downward, "pcol") + collect(band_piece, "pcol", 0)
         band_answer = backward_block(band_inverse[0], band_solved, band_back)
         outer = (
             multiply(to_band, band_answer, "aij,ir->ajr")

time: 1180 us -> 1230 us (1.042); the launches traced: 1180 us -> 1220 us
  starting transfers between devices: 0.33 us -> 60.5 us
  local copies, waits for them, and re-layouts: 23.6 us -> 69.9 us
  blocking collectives: 46 us -> 0 us
  waiting for transfers between devices: 999 us -> 979 us
    ppermute x0 -> x30, starting transfers between devices: none -> 60.1 us  [the longest x14 59.5 us: collect(): lax.ppermute(going_down, axis, [(d, (d - 1) % ways) for d in range(ways)])]
    psum x2, waiting for transfers between devices: 125 us -> 75.6 us  [per_device(): band_back = lax.psum(downward, 'pcol') + collect(band_piece, 'pcol', 0)]
    dynamic_update_slice x0 -> x32, local copies, waits for them, and re-layouts: none -> 47.1 us  [the longest x16 23.8 us: collect(): lax.dynamic_update_slice_in_dim(full, going_up, (here - far) % ways * ste...]
    all_gather x2 -> x0, blocking collectives: 46 us -> none  [per_device(): lax.all_gather(band_piece, 'pcol', axis=0, tiled=True)]
    ppermute x0 -> x30, waiting for transfers between devices: none -> 22.5 us  [the longest x16 21.4 us: collect(): lax.ppermute(going_up, axis, [(d, (d + 1) % ways) for d in range(ways)])]
  transfers between devices with their start and end apart: 8 -> 38, of which waited for: 8 -> 24; matrix products, arithmetic and copies ran while one was open for 2% -> 6% of each run, Pallas kernels for 0% -> 0%
where the time goes in v1:
time: 1230 us; the launch traced here: 1220 us
  waiting for transfers between devices  979 us (80%)
  matrix products  89.9 us (7%)
  local copies, waits for them, and re-layouts  69.9 us (6%)
  starting transfers between devices  60.5 us (5%)
  between operations  16.6 us (1%)
    psum x2, waiting for transfers between devices, per_device(): lax.psum(summit_term + multiply(own_lift, own_strip, 'ki,kn->in'), ('prow...  489 us
    psum x2, waiting for transfers between devices, per_device(): strip_partial = lax.psum(strip_term, 'prow')  211 us
    psum x2, waiting for transfers between devices, per_device(): band_partial = lax.psum(band_term, 'pcol')  181 us
    dot_general x76, matrix products, multiply(): return jnp.einsum(form, left, right, preferred_element_type=jnp.float32)  89.9 us
    psum x2, waiting for transfers between devices, per_device(): band_back = lax.psum(downward, 'pcol') + collect(band_piece, 'pcol', 0)  75.6 us
    ppermute x14, starting transfers between devices, collect(): lax.ppermute(going_down, axis, [(d, (d - 1) % ways) for d in range(ways)])  59.5 us
  transfers between devices with their start and end apart: 38, of which 24 were waited for; matrix products, arithmetic and copies ran while one was open for 6% of the time, Pallas kernels for 0%

profile of v1, /device:TPU:2, one launch (start us, length us, event | category | flops | bytes accessed | tf_op | source)
XLA Modules:
  0.0 1219.3 jit_solution(8205366531008388838)
XLA Ops:
  17.6 2.0 constant_dynamic-update-slice_fusion.15
  19.7 2.1 constant_dynamic-update-slice_fusion.14
  21.8 2.2 constant_dynamic-update-slice_fusion.13
  25.0 2.5 constant_dynamic-update-slice_fusion.12
  28.3 2.6 constant_dynamic-update-slice_fusion.11
  30.9 2.6 constant_dynamic-update-slice_fusion.18
  33.5 2.2 convolution_bitcast_fusion.19
  35.8 2.1 convolution_bitcast_fusion.18
  37.9 2.1 convolution_bitcast_fusion.17
  40.0 90.9 %all-reduce.9.cloned.1.call-done = f32[256,128]{1,0:T(8,128)} async-done(((f32[256,128]{1,0:T(8,128)}), f32[256,128]{1,0:T(8,128)}) %all-reduce.9.cloned.1.call-update) | async-done | bytes 131088 | tf_op jit(solution)/shard_map/psum | solution.py:140
  136.4 105.3 %all-reduce.11.cloned.1.call-done = f32[256,128]{1,0:T(8,128)} async-done(((f32[256,128]{1,0:T(8,128)}), f32[256,128]{1,0:T(8,128)}) %all-reduce.11.cloned.1.call-update) | async-done | bytes 131088 | tf_op jit(solution)/shard_map/psum | solution.py:145
  246.6 243.6 %all-reduce.13.cloned.1.call-done = f32[256,128]{1,0:T(8,128)} async-done(((f32[256,128]{1,0:T(8,128)}), f32[256,128]{1,0:T(8,128)}) %all-reduce.13.cloned.1.call-update) | async-done | bytes 131088 | tf_op jit(solution)/shard_map/psum | solution.py:149
  494.4 4.1 collective-permute-start.1
  500.8 4.2 collective-permute-start.3
  507.2 4.2 collective-permute-start.5
  513.5 4.4 collective-permute-start.7
  521.3 4.6 collective-permute-start.9
  528.1 4.5 collective-permute-start.11
  534.8 4.5 collective-permute-start.13
  567.0 56.4 %all-reduce.15.cloned.1.call-done = f32[256,128]{0,1:T(8,128)} async-done(((f32[256,128]{0,1:T(8,128)}), f32[256,128]{0,1:T(8,128)}) %all-reduce.15.cloned.1.call-update) | async-done | bytes 131088 | tf_op jit(solution)/shard_map/psum | solution.py:161
  635.5 2.1 constant_dynamic-update-slice_fusion.42
  637.6 2.2 constant_dynamic-update-slice_fusion.41
  639.9 2.4 constant_dynamic-update-slice_fusion.40
  642.2 2.4 constant_dynamic-update-slice_fusion.39
  644.6 2.5 constant_dynamic-update-slice_fusion.38
  647.1 2.6 constant_dynamic-update-slice_fusion.37
  649.7 2.7 constant_dynamic-update-slice_fusion.44
  652.4 2.2 convolution_bitcast_fusion.15
  654.6 2.2 convolution_bitcast_fusion.14
  656.8 2.2 convolution_bitcast_fusion.13
  659.0 89.7 %all-reduce.17.cloned.1.call-done = f32[256,128]{0,1:T(8,128)} async-done(((f32[256,128]{0,1:T(8,128)}), f32[256,128]{0,1:T(8,128)}) %all-reduce.17.cloned.1.call-update) | async-done | bytes 131088 | tf_op jit(solution)/shard_map/psum | solution.py:140
  754.1 105.4 %all-reduce.19.cloned.1.call-done = f32[256,128]{0,1:T(8,128)} async-done(((f32[256,128]{0,1:T(8,128)}), f32[256,128]{0,1:T(8,128)}) %all-reduce.19.cloned.1.call-update) | async-done | bytes 131088 | tf_op jit(solution)/shard_map/psum | solution.py:145
  863.2 245.8 %all-reduce.21.cloned.1.call-done = f32[256,128]{0,1:T(8,128)} async-done(((f32[256,128]{0,1:T(8,128)}), f32[256,128]{0,1:T(8,128)}) %all-reduce.21.cloned.1.call-update) | async-done | bytes 131088 | tf_op jit(solution)/shard_map/psum | solution.py:149
  1114.1 4.1 collective-permute-start.16
  1118.3 2.2 collective-permute-done.15
  1120.5 4.1 collective-permute-start.18
  1124.7 2.3 collective-permute-done.17
  1127.0 4.1 collective-permute-start.20
  1131.1 2.2 collective-permute-done.19
  1133.3 4.1 collective-permute-start.22
  1137.5 2.9 collective-permute-done.21
  1140.4 4.1 collective-permute-start.24
  1144.5 2.2 collective-permute-done.23
  1146.8 4.2 collective-permute-start.26
  1150.9 2.2 collective-permute-done.25
  1153.2 4.3 collective-permute-start.28
  1157.4 2.2 collective-permute-done.27
  1182.8 19.2 %all-reduce.23.cloned.1.call-done = f32[256,128]{0,1:T(8,128)} async-done(((f32[256,128]{0,1:T(8,128)}), f32[256,128]{0,1:T(8,128)}) %all-reduce.23.cloned.1.call-update) | async-done | bytes 131088 | tf_op jit(solution)/shard_map/psum | solution.py:161
  (389 shorter events, 126.7 us)
Async XLA Ops:
  7.2 26.3 %copy-start = (bf16[1,1,8,256,256]{4,3,2,1,0:T(8,128)(2,1)S(1)}, bf16[1,1,8,256,256]{4,3,2,1,0:T(8,128)(2,1)}, u32[]{:S(2)}) copy-start(bf16[1,1,8,256,256]{4,3,2,1,0:T(8,128)(2,1)} %param.54) | copy-start | bytes 3145732
  7.2 123.7 %all-reduce.9.cloned.1.call-start = ((), (), s32[]{:S(2)}) async-start(), calls=%async_computation | async-start | bytes 262144 | tf_op jit(solution)/shard_map/psum | solution.py:140
  30.9 101.8 %copy-start.9 = (bf16[1,1,256,256]{3,2,1,0:T(8,128)(2,1)S(1)}, bf16[1,1,256,256]{3,2,1,0:T(8,128)(2,1)}, u32[]{:S(2)}) copy-start(bf16[1,1,256,256]{3,2,1,0:T(8,128)(2,1)} %param.57) | copy-start | bytes 393220
  33.5 101.0 %copy-start.26 = (bf16[1,16,256]{2,1,0:T(8,128)(2,1)S(1)}, bf16[1,16,256]{2,1,0:T(8,128)(2,1)}, u32[]{:S(2)}) copy-start(bf16[1,16,256]{2,1,0:T(8,128)(2,1)} %param.58) | copy-start | bytes 24580
  33.5 208.2 %copy-start.8 = (bf16[1,256,256]{2,1,0:T(8,128)(2,1)S(1)}, bf16[1,256,256]{2,1,0:T(8,128)(2,1)}, u32[]{:S(2)}) copy-start(bf16[1,256,256]{2,1,0:T(8,128)(2,1)} %param.51) | copy-start | bytes 393220
  33.5 456.7 %copy-start.10 = (bf16[256,256]{1,0:T(8,128)(2,1)S(1)}, bf16[256,256]{1,0:T(8,128)(2,1)}, u32[]{:S(2)}) copy-start(bf16[256,256]{1,0:T(8,128)(2,1)} %param.52) | copy-start | bytes 393220
  35.7 206.0 %all-reduce.11.cloned.1.call-start = ((), (), s32[]{:S(2)}) async-start(), calls=%async_computation.1 | async-start | bytes 262144 | tf_op jit(solution)/shard_map/psum | solution.py:145
  134.5 355.8 %all-reduce.13.cloned.1.call-start = ((), (), s32[]{:S(2)}) async-start(), calls=%async_computation.2 | async-start | bytes 262144 | tf_op jit(solution)/shard_map/psum | solution.py:149
  245.3 378.1 %all-reduce.15.cloned.1.call-start = ((), (), s32[]{:S(2)}) async-start(), calls=%async_computation.3 | async-start | bytes 262144 | tf_op jit(solution)/shard_map/psum | solution.py:161
  493.1 6.5 collective-permute-start
  494.4 6.4 collective-permute-start.1
  499.5 6.4 collective-permute-start.2
  500.8 6.4 collective-permute-start.3
  505.9 6.4 collective-permute-start.4
  507.2 6.3 collective-permute-start.5
  512.3 7.1 collective-permute-start.6
  513.5 7.8 collective-permute-start.7
  519.4 6.7 collective-permute-start.8
  521.3 6.8 collective-permute-start.9
  526.1 6.7 collective-permute-start.10
  527.8 220.9 %all-reduce.17.cloned.1.call-start = ((), (), s32[]{:S(2)}) async-start(), calls=%async_computation.4 | async-start | bytes 262144 | tf_op jit(solution)/shard_map/psum | solution.py:140
  528.1 6.7 collective-permute-start.11
  532.8 6.7 collective-permute-start.12
  534.8 28.9 %collective-permute-start.13 = (f32[16,128]{0,1:T(8,128)}, f32[16,128]{0,1:T(8,128)}, u32[]{:S(2)}, u32[]{:S(2)}) collective-permute-start(f32[16,128]{0,1:T(8,128)} %collective-permute-done.11), channel_id=1, source_target_pairs={{0,15},{1,0},{2,1},{3,2},{4,3},{5,4},{6,5},{7,6},{8,7},{9,8},{10,9... | collective-permute-start | bytes 24584 | tf_op jit(solution)/shard_map/ppermute | solution.py:20
  539.5 25.9 %collective-permute-start.14 = (f32[16,128]{0,1:T(8,128)}, f32[16,128]{0,1:T(8,128)}, u32[]{:S(2)}, u32[]{:S(2)}) collective-permute-start(f32[16,128]{0,1:T(8,128)} %collective-permute-done.12), channel_id=1, source_target_pairs={{0,1},{1,2},{2,3},{3,4},{4,5},{5,6},{6,7},{7,8},{8,9},{9,10},{10,1... | collective-permute-start | bytes 24584 | tf_op jit(solution)/shard_map/ppermute | solution.py:17
  656.7 202.8 %all-reduce.19.cloned.1.call-start = ((), (), s32[]{:S(2)}) async-start(), calls=%async_computation.5 | async-start | bytes 262144 | tf_op jit(solution)/shard_map/psum | solution.py:145
  752.3 356.7 %all-reduce.21.cloned.1.call-start = ((), (), s32[]{:S(2)}) async-start(), calls=%async_computation.6 | async-start | bytes 262144 | tf_op jit(solution)/shard_map/psum | solution.py:149
  863.1 338.8 %all-reduce.23.cloned.1.call-start = ((), (), s32[]{:S(2)}) async-start(), calls=%async_computation.7 | async-start | bytes 262144 | tf_op jit(solution)/shard_map/psum | solution.py:161
  1113.9 6.6 collective-permute-start.15
  1114.1 6.4 collective-permute-start.16
  1120.5 6.4 collective-permute-start.17
  1120.5 6.4 collective-permute-start.18
  1126.9 32.7 %copy-start.32 = (f32[16,128]{0,1:T(8,128)}, f32[16,128]{0,1:T(8,128)S(1)}, u32[]{:S(2)}) copy-start(f32[16,128]{0,1:T(8,128)S(1)} %collective-permute-done.17) | copy-start | bytes 24580
  1126.9 6.4 collective-permute-start.19
  1127.0 32.7 %copy-start.33 = (f32[16,128]{0,1:T(8,128)}, f32[16,128]{0,1:T(8,128)S(1)}, u32[]{:S(2)}) copy-start(f32[16,128]{0,1:T(8,128)S(1)} %collective-permute-done.18) | copy-start | bytes 24580
  1127.0 6.4 collective-permute-start.20
  1133.3 26.3 %copy-start.34 = (f32[16,128]{0,1:T(8,128)}, f32[16,128]{0,1:T(8,128)S(1)}, u32[]{:S(2)}) copy-start(f32[16,128]{0,1:T(8,128)S(1)} %collective-permute-done.19) | copy-start | bytes 24580
  1133.3 7.1 collective-permute-start.21
  1133.3 26.3 %copy-start.35 = (f32[16,128]{0,1:T(8,128)}, f32[16,128]{0,1:T(8,128)S(1)}, u32[]{:S(2)}) copy-start(f32[16,128]{0,1:T(8,128)S(1)} %collective-permute-done.20) | copy-start | bytes 24580
  1133.3 7.0 collective-permute-start.22
  1140.4 6.4 collective-permute-start.23
  1140.4 6.4 collective-permute-start.24
  1146.8 6.4 collective-permute-start.25
  1146.8 6.4 collective-permute-start.26
  1153.2 6.5 collective-permute-start.27
  1153.2 26.9 %collective-permute-start.28 = (f32[16,128]{0,1:T(8,128)}, f32[16,128]{0,1:T(8,128)}, u32[]{:S(2)}, u32[]{:S(2)}) collective-permute-start(f32[16,128]{0,1:T(8,128)} %collective-permute-done.26), channel_id=1, source_target_pairs={{0,15},{1,0},{2,1},{3,2},{4,3},{5,4},{6,5},{7,6},{8,7},{9,8},{10,9... | collective-permute-start | bytes 24584 | tf_op jit(solution)/shard_map/ppermute | solution.py:20
  1159.7 21.7 %collective-permute-start.29 = (f32[16,128]{0,1:T(8,128)}, f32[16,128]{0,1:T(8,128)}, u32[]{:S(2)}, u32[]{:S(2)}) collective-permute-start(f32[16,128]{0,1:T(8,128)} %collective-permute-done.27), channel_id=1, source_target_pairs={{0,1},{1,2},{2,3},{3,4},{4,5},{5,6},{6,7},{7,8},{8,9},{9,10},{10,1... | collective-permute-start | bytes 24584 | tf_op jit(solution)/shard_map/ppermute | solution.py:17
  1167.8 36.0 %copy-start.11 = (bf16[128,256]{1,0:T(8,128)(2,1)S(1)}, bf16[128,256]{1,0:T(8,128)(2,1)}, u32[]{:S(2)}) copy-start(bf16[128,256]{1,0:T(8,128)(2,1)} %convolution_convert_fusion.2) | copy-start | bytes 196612
  (90 other events, 420.9 us)
Sparse Core Ops, SparseCore 0:
  35.8 95.0 all-reduce.8
  134.6 107.0 all-reduce.10
  247.8 242.3 all-reduce.12
  527.9 95.4 all-reduce.14
  656.9 91.7 all-reduce.16
  752.4 107.1 all-reduce.18
  866.6 242.3 all-reduce.20
  1113.1 88.8 all-reduce.22
